TPU v7x, 512 devices: a whole 4x8x8 slice. The times are simulated.
512 devices in a mesh: row: 64 (over y_lo, z, core), col: 8 (over y_hi, x).
Axes of the slice: x: 4, y: 8 (y_hi: 2, y_lo: 4; y = y_hi * 4 + y_lo), z: 8, core: 2. Of those that a mesh axis runs over, the one named last changes fastest.
Arguments:
- vectors: float32 [32768, 1024], P('row', 'col'), may hold values from -6 to 6
- householder: float32 [2, 32768, 256], P(None, 'row', 'col'), may hold values from -0.03125 to 0.03125
- tfactors: float32 [2, 256, 256], P(None, None, 'col'), may hold values from -0.17 to 2, as said below
Outputs:
- transformed: float32 [32768, 1024], P('row', 'col')
Inputs may be any that keep to these rules, and one draw needn't show every extreme that they name: Each tfactors[b] is upper triangular with a positive diagonal between 1 and 2.
All inputs are finite; a program needn't handle non-finite values.
Results may differ from a plain program's by a relative error of at most 0.0001.
Values sent between devices are 32-bit elements; how exact they have to be, the bound alone decides.
A program may use at most 64 MiB of HBM per device.

v0:
```python
import jax
import jax.numpy as jnp
from jax import lax
from jax.sharding import PartitionSpec as P

BLOCKS = 2


def turned_gather(arrays, axis, dims):
    turned = [jnp.moveaxis(a, dim, 0) for a, dim in zip(arrays, dims)]
    both = jnp.concatenate([t.reshape(len(t), -1) for t in turned], axis=1)
    whole, at, finished = (lax.all_gather(both, axis, axis=0, tiled=True), 0, [])
    for t, dim in zip(turned, dims):
        section = whole[:, at : at + t[0].size].reshape(-1, *t.shape[1:])
        finished.append(jnp.moveaxis(section, 0, dim))
        at += t[0].size
    return tuple(finished)


def split_up(value, dim, length):
    before, after = (value.shape[:dim], value.shape[dim + 1 :])
    return jnp.moveaxis(value.reshape(*before, length, -1, *after), dim, 0)


def summed_on_arrival(value, axis, dim):
    length = lax.axis_size(axis)
    tiles = lax.all_to_all(split_up(value, dim, length), axis, 0, 0, tiled=True)
    return jnp.sum(tiles, axis=0)


def joined_along(tiles, dim):
    lengths = list(tiles.shape[1:])
    lengths[dim] *= tiles.shape[0]
    return jnp.moveaxis(tiles, 0, dim).reshape(lengths)


def copy_for_each(value, axis):
    copies = jnp.broadcast_to(value, (lax.axis_size(axis), *value.shape))
    return lax.all_to_all(copies, axis, split_axis=0, concat_axis=0, tiled=True)


def collect(value, axis, dim):
    return joined_along(copy_for_each(value, axis), dim)


def project(current, blockv):
    return lax.dot_general(
        current,
        blockv,
        (((0,), (0,)), ((), ())),
        precision=lax.Precision.HIGHEST,
        preferred_element_type=jnp.float32,
    )


def apply_factor(products_t, blockt):
    return lax.dot_general(
        products_t,
        blockt,
        (((1,), (1,)), ((), ())),
        precision=lax.Precision.HIGHEST,
        preferred_element_type=jnp.float32,
    )


def on_device(vectors, householder, tfactors):
    current = vectors
    for block in range(BLOCKS):
        blockv, blockt = turned_gather((householder[block], tfactors[block]), "col", (1, 1))
        source = current
        shares = summed_on_arrival(project(source, blockv), "row", 0)
        reflect_share = apply_factor(shares, blockt)
        reflect_t = collect(reflect_share, "row", 0)
        current = current - lax.dot_general(
            blockv,
            reflect_t,
            (((1,), (1,)), ((), ())),
            precision=lax.Precision.HIGHEST,
            preferred_element_type=jnp.float32,
        )
    return current


def solution(mesh):
    return jax.shard_map(
        on_device,
        mesh=mesh,
        in_specs=(P("row", "col"), P(None, "row", "col"), P(None, None, "col")),
        out_specs=P("row", "col"),
        check_vma=False,
    )
```

profile of v0, /device:TPU:1, one launch (start us, length us, event | category | flops | bytes accessed | tf_op | source)
XLA Modules:
  0.0 163.8 jit_solution(3380706604660088206)
XLA Ops:
  0.0 0.8 slice_bitcast_fusion.2
  0.8 0.1 copy-done.1
  1.0 0.0 copy-start
  1.0 45.1 %all_gather.6 = f32[256,768]{1,0:T(8,128)S(1)} all-gather(f32[32,768]{1,0:T(8,128)S(1)} %pad_maximum_fusion), channel_id=1, replica_groups=mesh['row'=64,'col'=8] {'col'}, dimensions={0}, use_global_device_ids=true | all-gather | bytes 884736 | tf_op jit(solution)/shard_map/all_gather | solution.py:12
  46.1 0.6 convolution_bitcast_fusion
  46.7 0.7 reshape.12
  47.5 15.6 %all-to-all-start = ((f32[64,2,256]{2,1,0:T(2,128)}), f32[64,2,256]{2,1,0:T(2,128)S(1)}, u32[]{:S(2)}, u32[]{:S(2)}) async-start(f32[64,2,256]{2,1,0:T(2,128)} %reshape.12), calls=%async_computation | async-start | bytes 262144 | tf_op jit(solution)/shard_map/all_to_all | solution.py:27
  63.1 10.0 %all-to-all-done = f32[64,2,256]{2,1,0:T(2,128)S(1)} async-done(((f32[64,2,256]{2,1,0:T(2,128)}), f32[64,2,256]{2,1,0:T(2,128)S(1)}, u32[]{:S(2)}, u32[]{:S(2)}) %all-to-all-start) | async-done | bytes 131104 | tf_op jit(solution)/shard_map/all_to_all | solution.py:27
  73.0 0.1 reduce_sum.18
  73.1 0.2 fusion.7
  73.3 0.7 broadcast_in_dim.6
  74.0 5.0 %all-to-all-start.1 = ((f32[64,2,256]{2,1,0:T(2,128)}), f32[64,2,256]{2,1,0:T(2,128)S(1)}, u32[]{:S(2)}, u32[]{:S(2)}) async-start(f32[64,2,256]{2,1,0:T(2,128)} %broadcast_in_dim.6), calls=%async_computation.1 | async-start | bytes 262144 | tf_op jit(solution)/shard_map/all_to_all | solution.py:39
  79.0 40.2 %all_gather.7 = f32[256,768]{1,0:T(8,128)S(1)} all-gather(f32[32,768]{1,0:T(8,128)S(1)} %pad_maximum_fusion.1), channel_id=1, replica_groups=mesh['row'=64,'col'=8] {'col'}, dimensions={0}, use_global_device_ids=true | all-gather | bytes 884736 | tf_op jit(solution)/shard_map/all_gather | solution.py:12
  119.2 0.1 reshape.13
  119.3 1.0 convolution_subtract_fusion.1
  120.3 0.6 fusion.1
  120.9 0.1 reshape.14
  121.0 26.1 %all_to_all.20 = f32[64,2,256]{2,1,0:T(2,128)S(1)} all-to-all(f32[64,2,256]{2,1,0:T(2,128)S(1)} %reshape.14), channel_id=1, replica_groups=mesh['row'=64,'col'=8] {'row'}, dimensions={0} | all-to-all | bytes 262144 | tf_op jit(solution)/shard_map/all_to_all | solution.py:27
  147.1 0.1 reduce_sum.19
  147.1 0.2 fusion.5
  147.3 0.1 broadcast_in_dim.7
  147.4 14.6 %all_to_all.21 = f32[64,2,256]{2,1,0:T(2,128)S(1)} all-to-all(f32[64,2,256]{2,1,0:T(2,128)S(1)} %broadcast_in_dim.7), channel_id=1, replica_groups=mesh['row'=64,'col'=8] {'row'}, dimensions={0} | all-to-all | bytes 262144 | tf_op jit(solution)/shard_map/all_to_all | solution.py:39
  162.0 0.1 reshape.15
  162.1 1.7 %convolution_subtract_fusion = f32[512,128]{1,0:T(8,128)} fusion(f32[512,128]{1,0:T(8,128)S(1)} %convolution_subtract_fusion.1, f32[128,256]{1,0:T(8,128)S(1)} %reshape.15, f32[256,768]{1,0:T(8,128)S(1)} %all_gather.7), kind=kOutput, calls=%fused_computation | convolution fusion | flops 201392128 | bytes 1179648 | tf_op jit(solution)/shard_map/dot_general | solution.py:74
  (6 shorter events, 0.0 us)
Async XLA Ops:
  0.0 0.9 copy-start.1
  1.0 45.2 %copy-start = (f32[512,128]{1,0:T(8,128)S(1)}, f32[512,128]{1,0:T(8,128)}, u32[]{:S(2)}) copy-start(f32[512,128]{1,0:T(8,128)} %param.3) | copy-start | bytes 786436
  47.5 25.6 %all-to-all-start = ((f32[64,2,256]{2,1,0:T(2,128)}), f32[64,2,256]{2,1,0:T(2,128)S(1)}, u32[]{:S(2)}, u32[]{:S(2)}) async-start(f32[64,2,256]{2,1,0:T(2,128)} %reshape.12), calls=%async_computation | async-start | bytes 262144 | tf_op jit(solution)/shard_map/all_to_all | solution.py:27
  74.0 45.2 %all-to-all-start.1 = ((f32[64,2,256]{2,1,0:T(2,128)}), f32[64,2,256]{2,1,0:T(2,128)S(1)}, u32[]{:S(2)}, u32[]{:S(2)}) async-start(f32[64,2,256]{2,1,0:T(2,128)} %broadcast_in_dim.6), calls=%async_computation.1 | async-start | bytes 262144 | tf_op jit(solution)/shard_map/all_to_all | solution.py:39
where the time goes:
time: 164 us
  blocking collectives  126 us (77%)
  starting transfers between devices  20.6 us (13%)
  waiting for transfers between devices  9.97 us (6%)
  matrix products  4.25 us (3%)
  local copies, waits for them, and re-layouts  2.75 us (2%)
    all_gather x2, blocking collectives, turned_gather(): lax.all_gather(both, axis, axis=0, tiled=True)  85.3 us
    all_to_all x1, blocking collectives, summed_on_arrival(): tiles = lax.all_to_all(split_up(value, dim, length), axis, 0, 0, tiled=True)  26.1 us
    all_to_all x1, starting transfers between devices, summed_on_arrival(): tiles = lax.all_to_all(split_up(value, dim, length), axis, 0, 0, tiled=True)  15.6 us
    all_to_all x1, blocking collectives, copy_for_each(): return lax.all_to_all(copies, axis, split_axis=0, concat_axis=0, tiled=True)  14.6 us
    all_to_all x1, waiting for transfers between devices, summed_on_arrival(): tiles = lax.all_to_all(split_up(value, dim, length), axis, 0, 0, tiled=True)  9.97 us
    all_to_all x1, starting transfers between devices, copy_for_each(): return lax.all_to_all(copies, axis, split_axis=0, concat_axis=0, tiled=True)  4.96 us
  transfers between devices with their start and end apart: 2, of which 1 were waited for; matrix products, arithmetic and copies ran while one was open for 0% of the time, Pallas kernels for 0%

commit v1 on v0

--- a/solution.py
+++ b/solution.py
@@ -6,10 +6,17 @@
 BLOCKS = 2
 
 
+def gather_over(array, axis, d):
+    count = lax.axis_size(axis)
+    blocks = jnp.stack([array for _ in range(count)])
+    blocks = lax.all_to_all(blocks, axis, split_axis=0, concat_axis=0)
+    return jnp.concatenate(blocks, axis=d)
+
+
 def turned_gather(arrays, axis, dims):
     turned = [jnp.moveaxis(a, dim, 0) for a, dim in zip(arrays, dims)]
     both = jnp.concatenate([t.reshape(len(t), -1) for t in turned], axis=1)
-    whole, at, finished = (lax.all_gather(both, axis, axis=0, tiled=True), 0, [])
+    whole, at, finished = (gather_over(both, axis, 0), 0, [])
     for t, dim in zip(turned, dims):
         section = whole[:, at : at + t[0].size].reshape(-1, *t.shape[1:])
         finished.append(jnp.moveaxis(section, 0, dim))

time: 164 us -> 136 us (0.83)
  blocking collectives: 126 us -> 95.3 us
  waiting for transfers between devices: 9.97 us -> 23.9 us
  starting transfers between devices: 20.6 us -> 8.51 us
    all_gather x2 -> x0, blocking collectives: 85.3 us -> none  [turned_gather(): lax.all_gather(both, axis, axis=0, tiled=True)]
    all_to_all x1 -> x2, blocking collectives: 26.1 us -> 53.5 us  [summed_on_arrival(): tiles = lax.all_to_all(split_up(value, dim, length), axis, 0, 0, tiled=True)]
    all_to_all x0 -> x1, blocking collectives: none -> 27.2 us  [gather_over(): blocks = lax.all_to_all(blocks, axis, split_axis=0, concat_axis=0)]
    all_to_all x1, starting transfers between devices: 15.6 us -> 3.55 us  [gather_over(): blocks = lax.all_to_all(blocks, axis, split_axis=0, concat_axis=0)]
    all_to_all x1, waiting for transfers between devices: 0.01 us -> 10.1 us  [copy_for_each(): return lax.all_to_all(copies, axis, split_axis=0, concat_axis=0, tiled=True)]
    all_to_all x1, waiting for transfers between devices: 9.97 us -> 13.8 us  [gather_over(): blocks = lax.all_to_all(blocks, axis, split_axis=0, concat_axis=0)]
  transfers between devices with their start and end apart: 2 -> 2, of which waited for: 1 -> 2; matrix products, arithmetic and copies ran while one was open for 0% -> 1% of each run, Pallas kernels for 0% -> 0%
where the time goes in v1:
time: 136 us; the launch traced here: 135 us
  blocking collectives  95.3 us (70%)
  waiting for transfers between devices  23.9 us (18%)
  starting transfers between devices  8.51 us (6%)
  matrix products  4.24 us (3%)
  local copies, waits for them, and re-layouts  3.11 us (2%)
    all_to_all x2, blocking collectives, summed_on_arrival(): tiles = lax.all_to_all(split_up(value, dim, length), axis, 0, 0, tiled=True)  53.5 us
    all_to_all x1, blocking collectives, gather_over(): blocks = lax.all_to_all(blocks, axis, split_axis=0, concat_axis=0)  27.2 us
    all_to_all x1, blocking collectives, copy_for_each(): return lax.all_to_all(copies, axis, split_axis=0, concat_axis=0, tiled=True)  14.6 us
    all_to_all x1, waiting for transfers between devices, gather_over(): blocks = lax.all_to_all(blocks, axis, split_axis=0, concat_axis=0)  13.8 us
    all_to_all x1, waiting for transfers between devices, copy_for_each(): return lax.all_to_all(copies, axis, split_axis=0, concat_axis=0, tiled=True)  10.1 us
    all_to_all x1, starting transfers between devices, copy_for_each(): return lax.all_to_all(copies, axis, split_axis=0, concat_axis=0, tiled=True)  4.96 us
    all_to_all x1, starting transfers between devices, gather_over(): blocks = lax.all_to_all(blocks, axis, split_axis=0, concat_axis=0)  3.55 us
  transfers between devices with their start and end apart: 2, of which 2 were waited for; matrix products, arithmetic and copies ran while one was open for 1% of the time, Pallas kernels for 0%

profile of v1, /device:TPU:1, one launch (start us, length us, event | category | flops | bytes accessed | tf_op | source)
XLA Modules:
  0.0 135.3 jit_solution(13194665184520119837)
XLA Ops:
  0.0 0.8 slice_bitcast_fusion.2
  0.8 0.1 copy-done.1
  1.0 27.2 %all_to_all.30 = f32[8,32,768]{2,1,0:T(8,128)S(1)} all-to-all(f32[8,32,768]{2,1,0:T(8,128)S(1)} %stack.4), channel_id=1, replica_groups=mesh['row'=64,'col'=8] {'col'}, dimensions={0} | all-to-all | bytes 1572864 | tf_op jit(solution)/shard_map/all_to_all | solution.py:12
  28.3 0.6 convolution_bitcast_fusion
  28.9 0.1 reshape.23
  28.9 29.8 %all_to_all.31 = f32[64,2,256]{2,1,0:T(2,128)S(1)} all-to-all(f32[64,2,256]{2,1,0:T(2,128)S(1)} %reshape.23), channel_id=1, replica_groups=mesh['row'=64,'col'=8] {'row'}, dimensions={0} | all-to-all | bytes 262144 | tf_op jit(solution)/shard_map/all_to_all | solution.py:34
  58.8 0.1 reduce_sum.18
  58.9 0.2 fusion.7
  59.0 0.7 broadcast_in_dim.6
  59.8 5.0 %all-to-all-start.2 = ((f32[64,2,256]{2,1,0:T(2,128)}), f32[64,2,256]{2,1,0:T(2,128)S(1)}, u32[]{:S(2)}, u32[]{:S(2)}) async-start(f32[64,2,256]{2,1,0:T(2,128)} %broadcast_in_dim.6), calls=%async_computation.2 | async-start | bytes 262144 | tf_op jit(solution)/shard_map/all_to_all | solution.py:46
  64.8 10.1 %all-to-all-done.2 = f32[64,2,256]{2,1,0:T(2,128)S(1)} async-done(((f32[64,2,256]{2,1,0:T(2,128)}), f32[64,2,256]{2,1,0:T(2,128)S(1)}, u32[]{:S(2)}, u32[]{:S(2)}) %all-to-all-start.2) | async-done | bytes 131104 | tf_op jit(solution)/shard_map/all_to_all | solution.py:46
  74.9 1.0 stack.5
  75.8 3.5 %all-to-all-start.3 = ((f32[8,32,768]{2,1,0:T(8,128)}), f32[8,32,768]{2,1,0:T(8,128)S(1)}, u32[]{:S(2)}, u32[]{:S(2)}) async-start(f32[8,32,768]{2,1,0:T(8,128)} %stack.5), calls=%async_computation.3 | async-start | bytes 1572864 | tf_op jit(solution)/shard_map/all_to_all | solution.py:12
  79.4 0.1 reshape.24
  79.5 1.0 convolution_subtract_fusion.1
  80.5 13.8 %all-to-all-done.3 = f32[8,32,768]{2,1,0:T(8,128)S(1)} async-done(((f32[8,32,768]{2,1,0:T(8,128)}), f32[8,32,768]{2,1,0:T(8,128)S(1)}, u32[]{:S(2)}, u32[]{:S(2)}) %all-to-all-start.3) | async-done | bytes 786464 | tf_op jit(solution)/shard_map/all_to_all | solution.py:12
  94.2 0.6 fusion.1
  94.9 23.6 %all_to_all.32 = f32[64,2,256]{2,1,0:T(2,128)S(1)} all-to-all(f32[64,2,256]{2,1,0:T(2,128)S(1)} %reshape.26), channel_id=1, replica_groups=mesh['row'=64,'col'=8] {'row'}, dimensions={0} | all-to-all | bytes 262144 | tf_op jit(solution)/shard_map/all_to_all | solution.py:34
  118.5 0.1 reduce_sum.19
  118.6 0.2 fusion.5
  118.8 0.1 broadcast_in_dim.7
  118.9 14.6 %all_to_all.33 = f32[64,2,256]{2,1,0:T(2,128)S(1)} all-to-all(f32[64,2,256]{2,1,0:T(2,128)S(1)} %broadcast_in_dim.7), channel_id=1, replica_groups=mesh['row'=64,'col'=8] {'row'}, dimensions={0} | all-to-all | bytes 262144 | tf_op jit(solution)/shard_map/all_to_all | solution.py:46
  133.5 0.1 reshape.27
  133.6 1.7 %convolution_subtract_fusion = f32[512,128]{1,0:T(8,128)} fusion(f32[512,128]{1,0:T(8,128)S(1)} %convolution_subtract_fusion.1, f32[128,256]{1,0:T(8,128)S(1)} %reshape.27, f32[256,768]{1,0:T(8,128)S(1)} %bitcast.31), kind=kOutput, calls=%fused_computation | convolution fusion | flops 201392128 | bytes 1179648 | tf_op jit(solution)/shard_map/dot_general | solution.py:81
  (8 shorter events, 0.2 us)
Async XLA Ops:
  0.0 0.9 copy-start.1
  1.0 27.2 %copy-start = (f32[512,128]{1,0:T(8,128)S(1)}, f32[512,128]{1,0:T(8,128)}, u32[]{:S(2)}) copy-start(f32[512,128]{1,0:T(8,128)} %param.3) | copy-start | bytes 786436
  59.8 15.1 %all-to-all-start.2 = ((f32[64,2,256]{2,1,0:T(2,128)}), f32[64,2,256]{2,1,0:T(2,128)S(1)}, u32[]{:S(2)}, u32[]{:S(2)}) async-start(f32[64,2,256]{2,1,0:T(2,128)} %broadcast_in_dim.6), calls=%async_computation.2 | async-start | bytes 262144 | tf_op jit(solution)/shard_map/all_to_all | solution.py:46
  75.8 18.4 %all-to-all-start.3 = ((f32[8,32,768]{2,1,0:T(8,128)}), f32[8,32,768]{2,1,0:T(8,128)S(1)}, u32[]{:S(2)}, u32[]{:S(2)}) async-start(f32[8,32,768]{2,1,0:T(8,128)} %stack.5), calls=%async_computation.3 | async-start | bytes 1572864 | tf_op jit(solution)/shard_map/all_to_all | solution.py:12
